TPU v7x, 32 devices: a whole 2x2x4 slice. The times are simulated.
32 devices in a mesh: mol: 2 (over x), term: 16 (over z, y, core).
Axes of the slice: x: 2, y: 2, z: 4, core: 2. Of those that a mesh axis runs over, the one named last changes fastest.
Arguments:
- wave: bfloat16 [32, 2, 256, 256], P(('mol', 'term')), parts along dimension 0, may hold values from -6 to 6
- left_ops: bfloat16 [64, 24, 256, 256], P(('mol', 'term')), parts along dimension 0, may hold values from -0.375 to 0.375
- right_ops: bfloat16 [64, 24, 256, 256], P(('mol', 'term')), parts along dimension 0, may hold values from -0.375 to 0.375
- pair_src: int32 [64, 24], P(('mol', 'term')), parts along dimension 0, may hold values from 0 to 15
- pair_dst: int32 [64, 24], P(('mol', 'term')), parts along dimension 0, may hold values from 0 to 15
- sector_dims: int32 [2, 32], P(None, 'mol'), parts along dimension 1, may hold values from 128 to 256
Outputs:
- product: bfloat16 [32, 2, 256, 256], P(('mol', 'term')), parts along dimension 0
There are 2 independent parts, one for each index of `mol`. A program takes and returns all parts, laid end to end along the dimension named above; each array names one. Nothing has to cross between parts.
All inputs are finite; a program needn't handle non-finite values.
Results may differ from a plain program's by a relative error of at most 0.0049.
Values may be sent and summed in bfloat16 or wider, within the bound.
A program may use at most 128 MiB of HBM per device.

v0:
```python
import jax
import jax.numpy as jnp
from jax import lax
from jax.sharding import PartitionSpec as P


def sector_mask(sector_dims, size):
    rows = jnp.arange(size, dtype=jnp.int32)
    row_ok = (rows[None, :] < sector_dims[0][:, None]).astype(jnp.float32)
    col_ok = (rows[None, :] < sector_dims[1][:, None]).astype(jnp.float32)
    return row_ok[:, :, None] * col_ok[:, None, :]


def per_device(wave, left_ops, right_ops, pair_src, pair_dst, sector_dims):
    sec_own = wave.shape[0]
    width = wave.shape[2]
    gathered = lax.all_gather(wave, "term", axis=0, tiled=True)
    sectors = gathered.shape[0]
    mask = sector_mask(sector_dims, width)
    masked = (gathered.astype(jnp.float32) * mask[:, None]).astype(jnp.bfloat16)
    count = left_ops.shape[0] * left_ops.shape[1]
    lefts = left_ops.reshape(count, width, width)
    rights = right_ops.reshape(count, width, width)
    srcs = pair_src.reshape(-1)
    dsts = pair_dst.reshape(-1)
    picked = jnp.take(masked, srcs, axis=0)
    half = jnp.einsum("pij,pvjk->pvik", lefts, picked, preferred_element_type=jnp.float32).astype(
        jnp.bfloat16
    )
    full = jnp.einsum("pvik,plk->pvil", half, rights, preferred_element_type=jnp.float32)
    partial_sum = jax.ops.segment_sum(full, dsts, num_segments=sectors)
    totals = lax.psum(partial_sum, "term")
    first = lax.axis_index("term") * sec_own
    mine = lax.dynamic_slice_in_dim(totals, first, sec_own, 0)
    first_own = lax.axis_index("term") * sec_own
    own_mask = lax.dynamic_slice_in_dim(mask, first_own, sec_own, 0)
    return (mine * own_mask[:, None]).astype(jnp.bfloat16)


def solution(mesh):
    placed = (
        P(("mol", "term"), None, None, None),
        P(("mol", "term"), None, None, None),
        P(("mol", "term"), None, None, None),
        P(("mol", "term"), None),
        P(("mol", "term"), None),
        P(None, "mol"),
    )
    return jax.shard_map(
        per_device,
        mesh=mesh,
        in_specs=placed,
        out_specs=P(("mol", "term"), None, None, None),
        check_vma=False,
    )
```

profile of v0, /device:TPU:0, one launch (start us, length us, event | category | flops | bytes accessed | tf_op | source)
XLA Modules:
  0.0 333.4 jit_solution(8095929980802502439)
XLA Ops:
  6.5 0.0 all-gather.2.cloned.1.call-start
  6.5 0.7 all-gather.2.cloned.1.call-update
  7.3 0.0 all-reduce.2.cloned.1.call-start
  7.3 0.8 reshape.96
  8.1 0.8 reshape.95
  8.8 0.8 reshape.109
  9.6 0.8 slice_bitcast_fusion.1
  10.4 0.1 fusion.12
  10.4 2.3 broadcast_multiply_fusion
  12.7 50.1 %all-gather.2.cloned.1.call-done = bf16[16,2,256,256]{3,2,1,0:T(8,128)(2,1)} async-done(((bf16[1,2,256,256]{3,2,1,0:T(8,128)(2,1)}), bf16[16,2,256,256]{3,2,1,0:T(8,128)(2,1)}) %all-gather.2.cloned.1.call-update) | async-done | bytes 4194320 | tf_op jit(solution)/shard_map/all_gather | solution.py:17
  62.8 6.6 %multiply_convert_fusion = bf16[16,2,256,256]{3,2,1,0:T(8,128)(2,1)} fusion(bf16[16,2,256,256]{3,2,1,0:T(8,128)(2,1)} %all-gather.2.cloned.1.call-done, f32[16,256,256]{2,1,0:T(8,128)} %broadcast_multiply_fusion), kind=kLoop, calls=%fused_computation.8 | loop fusion | flops 6291456 | bytes 12582912 | tf_op jit(solution)/shard_map/convert_element_type | solution.py:20
  69.4 8.5 %gather_fusion = bf16[48,2,256,256]{3,2,1,0:T(8,128)(2,1)} fusion(bf16[16,2,256,256]{3,2,1,0:T(8,128)(2,1)} %multiply_convert_fusion, s32[1024]{0:T(1024)S(1)} %pad_clamp_fusion), kind=kCustom, calls=%fused_computation | custom fusion | bytes 25166016 | tf_op jit(solution)/shard_map/jit(_take)/gather | solution.py:26
  78.0 20.5 %fusion = f32[48,2,256,256]{3,2,1,0:T(8,128)} fusion(bf16[48,256,256,1]{2,1,3,0:T(8,128)(2,1)} %bitcast.23, bf16[48,256,256,1]{2,1,3,0:T(8,128)(2,1)} %bitcast.24, bf16[48,2,256,256]{3,2,1,0:T(8,128)(2,1)} %gather_fusion, pred[48]{0:T(512)(128)(4,1)S(1)} %compare_and_fusion), kind=kOutput, calls=%fused_computation.2 | convolution fusion | flops 6455033856 | bytes 50331696 | tf_op jit(solution)/shard_map/pvik,plk->pvil/dot_general | solution.py:30
  98.5 4.2 %broadcast_in_dim.12 = f32[16,2,256,256]{3,2,1,0:T(8,128)} broadcast(f32[]{:T(128)} %constant.7.clone.1), dimensions={} | broadcast | bytes 8388612 | tf_op jit(solution)/shard_map/broadcast_in_dim | solution.py:31
  102.7 53.0 %scatter_fusion = f32[16,2,256,256]{3,2,1,0:T(8,128)} fusion(f32[16,2,256,256]{3,2,1,0:T(8,128)} %broadcast_in_dim.12, s32[48]{0:T(128)S(1)} %reshape.109, f32[48,2,256,256]{3,2,1,0:T(8,128)} %fusion), kind=kCustom, calls=%fused_computation.1 | custom fusion | flops 6291456 | bytes 75497664 | tf_op jit(solution)/shard_map/scatter-add | solution.py:31
  155.7 0.0 all-reduce.2.cloned.1.call-update
  155.7 1.0 dynamic-slice_bitcast_fusion
  156.7 168.0 %all-reduce.2.cloned.1.call-done = f32[16,2,256,256]{3,2,1,0:T(8,128)} async-done(((f32[16,2,256,256]{3,2,1,0:T(8,128)}), f32[16,2,256,256]{3,2,1,0:T(8,128)}) %all-reduce.2.cloned.1.call-update) | async-done | bytes 8388624 | tf_op jit(solution)/shard_map/psum | solution.py:32
  324.7 1.8 multiply_convert_fusion.1
  (3 shorter events, 0.0 us)
Async XLA Ops:
  6.5 56.3 %all-gather.2.cloned.1.call-start = ((), (), s32[]{:S(2)}) async-start(), calls=%async_computation | async-start | bytes 4456448 | tf_op jit(solution)/shard_map/all_gather | solution.py:17
  7.3 317.5 %all-reduce.2.cloned.1.call-start = ((), (), s32[]{:S(2)}) async-start(), calls=%async_computation.1 | async-start | bytes 16777216 | tf_op jit(solution)/shard_map/psum | solution.py:32
Sparse Core Ops, SparseCore 0:
  9.5 53.2 all-gather.1
  155.8 168.8 all-reduce.1
where the time goes:
time: 334 us; the launch traced here: 333 us
  waiting for transfers between devices  219 us (66%)
  other arithmetic  63.8 us (19%)
  matrix products  20.5 us (6%)
  local copies, waits for them, and re-layouts  16.7 us (5%)
  between operations  13.4 us (4%)
    psum x1, waiting for transfers between devices, per_device(): totals = lax.psum(partial_sum, 'term')  168 us
    scatter-add x1, other arithmetic, per_device(): partial_sum = jax.ops.segment_sum(full, dsts, num_segments=sectors)  53 us
    all_gather x1, waiting for transfers between devices, per_device(): gathered = lax.all_gather(wave, 'term', axis=0, tiled=True)  50.1 us
    dot_general x1, matrix products, per_device(): jnp.einsum('pvik,plk->pvil', half, rights, preferred_element_type=jnp.flo...  20.5 us
    gather x1, local copies, waits for them, and re-layouts, per_device(): picked = jnp.take(masked, srcs, axis=0)  8.54 us
  transfers between devices with their start and end apart: 2, of which 2 were waited for; matrix products, arithmetic and copies ran while one was open for 2% of the time, Pallas kernels for 0%

commit v1 on v0

v1 whole, which is shorter than its diff:
```python
import functools

import jax
import jax.numpy as jnp
from jax import lax
from jax.experimental import pallas as pl
from jax.experimental.pallas import tpu as pltpu
from jax.sharding import PartitionSpec as P

MESH = pl.DeviceIdType.MESH
GROUP = 4


def chip_of(pos, chips):
    if chips == 8:
        back = pos // 4
        return 2 * (pos + back * (7 - 2 * pos)) + back
    return pos


def pos_of(chip, chips):
    if chips == 8:
        up, col = chip // 2, chip % 2
        return up + col * (7 - 2 * up)
    return chip


def places(chips):
    me = lax.axis_index("term")
    core = lax.rem(me, 2)
    pos = pos_of(me // 2, chips)

    def at(shift):
        return 2 * chip_of(lax.rem(pos + shift + chips, chips), chips) + core

    return me, core, at, me + 1 - 2 * core


def mask_of(dims_ref, sector, size):
    rows = lax.broadcasted_iota(jnp.int32, (size, size), 0)
    cols = lax.broadcasted_iota(jnp.int32, (size, size), 1)
    inside = (rows < dims_ref[0, sector]) & (cols < dims_ref[1, sector])
    return jnp.where(inside, 1.0, 0.0).astype(jnp.float32)


def greet(devices):
    barrier = pltpu.get_barrier_semaphore()
    for device in devices:
        pl.semaphore_signal(barrier, inc=1, device_id={"term": device}, device_id_type=MESH)
    pl.semaphore_wait(barrier, len(devices))


def reach(chips, way, v):
    return chips // 2 - (1 if way != v else 0)


def gather_kernel(chips, dims_ref, wave_ref, out_ref, own, local_sem, ring_send, ring_recv, sib_send, sib_recv):
    size = wave_ref.shape[-1]
    me, core, at, sib = places(chips)
    flip = 1 - 2 * core
    greet((at(1), at(-1), sib))
    mask = mask_of(dims_ref, me, size)
    waits = []
    half = chips // 2

    def ring(way, step, v, src, index):
        return pltpu.make_async_remote_copy(
            src_ref=src,
            dst_ref=out_ref.at[index, v],
            send_sem=ring_send.at[way, step, v],
            recv_sem=ring_recv.at[way, step, v],
            device_id={"term": at(1 - 2 * way)},
            device_id_type=MESH,
        )

    def sibling(way, step, v, src, index):
        return pltpu.make_async_remote_copy(
            src_ref=src,
            dst_ref=out_ref.at[index, v],
            send_sem=sib_send.at[way, step, v],
            recv_sem=sib_recv.at[way, step, v],
            device_id={"term": sib},
            device_id_type=MESH,
        )

    for v in range(2):
        own[v] = (wave_ref[0, v].astype(jnp.float32) * mask).astype(jnp.bfloat16)
        for way in range(2):
            copy = ring(way, 0, v, own.at[v], me)
            copy.start()
            waits.append(copy)
    for v in range(2):
        copy = sibling(0, half, v, own.at[v], me)
        copy.start()
        waits.append(copy)
        copy = pltpu.make_async_copy(own.at[v], out_ref.at[me, v], local_sem.at[v])
        copy.start()
        waits.append(copy)
    arrivals = []
    for step in range(half):
        for v in range(2):
            for way in range(2):
                if step >= reach(chips, way, v):
                    continue
                index = at(-(step + 1) * (1 - 2 * way))
                block = out_ref.at[index, v]
                ring(way, step, v, block, index).wait_recv()
                if step + 1 < reach(chips, way, v):
                    copy = ring(way, step + 1, v, block, index)
                    copy.start()
                    waits.append(copy)
                copy = sibling(way, step, v, block, index)
                copy.start()
                waits.append(copy)
                arrivals.append(sibling(way, step, v, block, index + flip))
    for v in range(2):
        arrivals.append(sibling(0, half, v, own.at[v], me + flip))
    for copy in arrivals:
        copy.wait_recv()
    for copy in waits:
        if hasattr(copy, "wait_send") and copy.is_remote:
            copy.wait_send()
        else:
            copy.wait()


def gather(chips, dims, wave):
    half = chips // 2
    size = wave.shape[-1]
    sems = pltpu.SemaphoreType.DMA((2, half + 1, 2))
    return pl.pallas_call(
        functools.partial(gather_kernel, chips),
        out_shape=jax.ShapeDtypeStruct((2 * chips, 2, size, size), jnp.bfloat16),
        in_specs=[pl.BlockSpec(memory_space=pltpu.SMEM), pl.BlockSpec(memory_space=pltpu.VMEM)],
        out_specs=pl.BlockSpec(memory_space=pl.ANY),
        scratch_shapes=[
            pltpu.VMEM((2, size, size), jnp.bfloat16),
            pltpu.SemaphoreType.DMA((2,)),
            sems,
            sems,
            sems,
            sems,
        ],
        compiler_params=pltpu.CompilerParams(
            collective_id=0, has_side_effects=True, vmem_limit_bytes=16 * 2**20
        ),
        name="gather",
    )(dims, wave)


def pairs_kernel(src_ref, dst_ref, left_ref, right_ref, wave_ref, out_ref, acc):
    step = pl.program_id(0)

    @pl.when(step == 0)
    def _():
        acc[...] = jnp.zeros_like(acc)

    for g in range(GROUP):
        src = src_ref[step * GROUP + g]
        dst = dst_ref[step * GROUP + g]
        left = left_ref[g]
        right = right_ref[g]
        for v in range(2):
            half = jnp.dot(left, wave_ref[src, v], preferred_element_type=jnp.float32).astype(jnp.bfloat16)
            acc[dst, v] += lax.dot_general(
                half, right, (((1,), (1,)), ((), ())), preferred_element_type=jnp.float32
            )

    @pl.when(step == pl.num_programs(0) - 1)
    def _():
        out_ref[...] = acc[...].astype(jnp.bfloat16)


def pairs(srcs, dsts, lefts, rights, gathered):
    count, size, _ = lefts.shape
    whole = lambda i, s, d: (0, 0, 0, 0)
    block = pl.BlockSpec((GROUP, size, size), lambda i, s, d: (i, 0, 0))
    return pl.pallas_call(
        pairs_kernel,
        out_shape=jax.ShapeDtypeStruct(gathered.shape, jnp.bfloat16),
        grid_spec=pltpu.PrefetchScalarGridSpec(
            num_scalar_prefetch=2,
            grid=(count // GROUP,),
            in_specs=[
                block,
                block,
                pl.BlockSpec(gathered.shape, whole, pipeline_mode=pl.Buffered(1)),
            ],
            out_specs=pl.BlockSpec(gathered.shape, whole, pipeline_mode=pl.Buffered(1)),
            scratch_shapes=[pltpu.VMEM(gathered.shape, jnp.float32)],
        ),
        compiler_params=pltpu.CompilerParams(vmem_limit_bytes=48 * 2**20),
        name="pairs",
    )(srcs, dsts, lefts, rights, gathered)


def scatter_kernel(chips, dims_ref, part_ref, out_ref, sent, came, shared, ring_send, ring_recv, sib_send, sib_recv):
    size = out_ref.shape[-1]
    me, core, at, sib = places(chips)
    flip = 1 - 2 * core
    greet((at(1), at(-1), sib))
    waits = []
    half = chips // 2

    def sibling(way, step, v, index):
        return pltpu.make_async_remote_copy(
            src_ref=part_ref.at[index + flip, v],
            dst_ref=shared.at[way, step, v],
            send_sem=sib_send.at[way, step, v],
            recv_sem=sib_recv.at[way, step, v],
            device_id={"term": sib},
            device_id_type=MESH,
        )

    def ring(way, step, v):
        return pltpu.make_async_remote_copy(
            src_ref=sent.at[way, step, v],
            dst_ref=came.at[way, step, v],
            send_sem=ring_send.at[way, step, v],
            recv_sem=ring_recv.at[way, step, v],
            device_id={"term": at(1 - 2 * way)},
            device_id_type=MESH,
        )

    plan = []
    for step in range(half):
        for v in range(2):
            for way in range(2):
                first = half - reach(chips, way, v)
                if step >= first:
                    index = at((half - step) * (1 - 2 * way))
                    plan.append((way, step, v, first, index))
    for way, step, v, first, index in plan:
        copy = sibling(way, step, v, index)
        copy.start()
        waits.append(copy)
    for v in range(2):
        copy = sibling(0, half, v, me)
        copy.start()
        waits.append(copy)
    for way, step, v, first, index in plan:
        sibling(way, step, v, index).wait_recv()
        total = part_ref[index, v].astype(jnp.float32) + shared[way, step, v].astype(jnp.float32)
        if step > first:
            ring(way, step - 1, v).wait_recv()
            total += came[way, step - 1, v].astype(jnp.float32)
        sent[way, step, v] = total.astype(jnp.bfloat16)
        copy = ring(way, step, v)
        copy.start()
        waits.append(copy)
    mask = mask_of(dims_ref, me, size)
    for v in range(2):
        sibling(0, half, v, me).wait_recv()
        total = part_ref[me, v].astype(jnp.float32) + shared[0, half, v].astype(jnp.float32)
        for way in range(2):
            ring(way, half - 1, v).wait_recv()
            total += came[way, half - 1, v].astype(jnp.float32)
        out_ref[0, v] = (total * mask).astype(jnp.bfloat16)
    for copy in waits:
        copy.wait_send()


def scatter(chips, dims, part):
    half = chips // 2
    size = part.shape[-1]
    sems = pltpu.SemaphoreType.DMA((2, half + 1, 2))
    return pl.pallas_call(
        functools.partial(scatter_kernel, chips),
        out_shape=jax.ShapeDtypeStruct((1, 2, size, size), jnp.bfloat16),
        in_specs=[pl.BlockSpec(memory_space=pltpu.SMEM), pl.BlockSpec(memory_space=pltpu.VMEM)],
        out_specs=pl.BlockSpec(memory_space=pltpu.VMEM),
        scratch_shapes=[
            pltpu.VMEM((2, half, 2, size, size), jnp.bfloat16),
            pltpu.VMEM((2, half, 2, size, size), jnp.bfloat16),
            pltpu.VMEM((2, half + 1, 2, size, size), jnp.bfloat16),
            sems,
            sems,
            sems,
            sems,
        ],
        compiler_params=pltpu.CompilerParams(
            collective_id=1, has_side_effects=True, vmem_limit_bytes=48 * 2**20
        ),
        name="scatter",
    )(dims, part)


def per_device(chips, wave, left_ops, right_ops, pair_src, pair_dst, sector_dims):
    size = wave.shape[-1]
    gathered = gather(chips, sector_dims, wave)
    part = pairs(
        pair_src.reshape(-1),
        pair_dst.reshape(-1),
        left_ops.reshape(-1, size, size),
        right_ops.reshape(-1, size, size),
        gathered,
    )
    return scatter(chips, sector_dims, part)


def solution(mesh):
    held = P(("mol", "term"), None, None, None)
    index = P(("mol", "term"), None)
    return jax.shard_map(
        functools.partial(per_device, mesh.shape["term"] // 2),
        mesh=mesh,
        in_specs=(held, held, held, index, index, P(None, "mol")),
        out_specs=held,
        check_vma=False,
    )
```

time: 334 us -> 79.8 us (0.24)
  waiting for transfers between devices: 219 us -> 0 us
  Pallas kernels: 0 us -> 73.5 us
  other arithmetic: 63.8 us -> 0 us
  matrix products: 20.5 us -> 0 us
  between operations: 13.4 us -> 0.04 us
  local copies, waits for them, and re-layouts: 16.7 us -> 5.79 us
    psum x1 -> x0, waiting for transfers between devices: 168 us -> none  [per_device(): totals = lax.psum(partial_sum, 'term')]
    pallas_call x0 -> x3, Pallas kernels: none -> 73.5 us  [the longest x1 29 us: gather(): pl.pallas_call(functools.partial(gather_kernel, chips), out_shape=jax.Sha...]
    scatter-add x1 -> x0, other arithmetic: 53 us -> none  [per_device(): partial_sum = jax.ops.segment_sum(full, dsts, num_segments=sectors)]
    all_gather x1 -> x0, waiting for transfers between devices: 50.1 us -> none  [per_device(): gathered = lax.all_gather(wave, 'term', axis=0, tiled=True)]
    dot_general x1 -> x0, matrix products: 20.5 us -> none  [per_device(): jnp.einsum('pvik,plk->pvil', half, rights, preferred_element_type=jnp.flo...]
    gather x1 -> x0, local copies, waits for them, and re-layouts: 8.54 us -> none  [per_device(): picked = jnp.take(masked, srcs, axis=0)]
    convert_element_type x3 -> x0, other arithmetic: 8.48 us -> none  [the longest x1 6.6 us: per_device(): masked = (gathered.astype(jnp.float32) * mask[:, None]).astype(jnp.bfloat16)]
    unnamed x0 -> x9, local copies, waits for them, and re-layouts: none -> 4.27 us
  transfers between devices with their start and end apart: 2 -> 0, of which waited for: 2 -> 0; matrix products, arithmetic and copies ran while one was open for 2% -> 0% of each run, Pallas kernels for 0% -> 0%
where the time goes in v1:
time: 79.8 us; the launch traced here: 79.4 us
  Pallas kernels  73.5 us (92%)
  local copies, waits for them, and re-layouts  5.79 us (7%)
    pallas_call x1, Pallas kernels, gather(): pl.pallas_call(functools.partial(gather_kernel, chips), out_shape=jax.Sha...  29 us
    pallas_call x1, Pallas kernels, scatter(): pl.pallas_call(functools.partial(scatter_kernel, chips), out_shape=jax.Sh...  28.4 us
    pallas_call x1, Pallas kernels, pairs(): pl.pallas_call(pairs_kernel, out_shape=jax.ShapeDtypeStruct(gathered.shap...  16.2 us
    unnamed x9, local copies, waits for them, and re-layouts  4.27 us

profile of v1, /device:TPU:0, one launch (start us, length us, event | category | flops | bytes accessed | tf_op | source)
XLA Modules:
  0.0 79.4 jit_solution(10722399978095059981)
XLA Ops:
  0.0 0.8 reshape.12.src_ref
  0.8 0.8 reshape.13.dst_ref
  1.5 0.0 copy-start.1
  1.5 0.9 %copy-done.1 = bf16[1,2,256,256]{3,2,1,0:T(8,128)(2,1)S(1)} copy-done((bf16[1,2,256,256]{3,2,1,0:T(8,128)(2,1)S(1)}, bf16[1,2,256,256]{3,2,1,0:T(8,128)(2,1)}, u32[]{:S(2)}) %copy-start.1) | copy-done | bytes 262168
  2.5 0.0 copy-start.2
  2.5 0.7 copy-done.2
  3.1 29.0 %gather.1.wave_ref = bf16[16,2,256,256]{3,2,1,0:T(8,128)(2,1)S(1)} custom-call(s32[2,16]{1,0:T(2,128)S(1)} %copy-done.2, bf16[1,2,256,256]{3,2,1,0:T(8,128)(2,1)S(1)} %copy-done.1), custom_call_target="tpu_custom_call" | custom-call | tf_op jit(solution)/shard_map/gather/pallas_call | solution.py:131
  32.2 0.0 copy-start
  32.2 1.9 %copy-done = bf16[16,2,256,256]{3,2,1,0:T(8,128)(2,1)} copy-done((bf16[16,2,256,256]{3,2,1,0:T(8,128)(2,1)}, bf16[16,2,256,256]{3,2,1,0:T(8,128)(2,1)S(1)}, u32[]{:S(2)}) %copy-start) | copy-done | bytes 4194328
  34.1 0.0 copy-start.3
  34.1 16.2 %pairs.1.part_ref = bf16[16,2,256,256]{3,2,1,0:T(8,128)(2,1)S(1)} custom-call(s32[48]{0:T(128)S(1)} %reshape.12.src_ref, s32[48]{0:T(128)S(1)} %reshape.13.dst_ref, bf16[48,256,256]{2,1,0:T(8,128)(2,1)} %bitcast.2, bf16[48,256,256]{2,1,0:T(8,128)(2,1)} %bitcast.3, bf16[16,2,256,256]{3,2,1,0:T(8,128)(2,1)} %copy-done), custom_call_target="tpu_custom_call" | custom-call | tf_op jit(solution)/shard_map/pairs/pallas_call | solution.py:178
  50.3 0.0 copy-done.3
  50.3 28.4 %scatter.1 = bf16[1,2,256,256]{3,2,1,0:T(8,128)(2,1)S(1)} custom-call(s32[2,16]{1,0:T(2,128)S(1)} %copy-done.3, bf16[16,2,256,256]{3,2,1,0:T(8,128)(2,1)S(1)} %pairs.1.part_ref), custom_call_target="tpu_custom_call" | custom-call | tf_op jit(solution)/shard_map/scatter/pallas_call | solution.py:267
  78.7 0.7 copy.8
Async XLA Ops:
  1.5 0.9 %copy-start.1 = (bf16[1,2,256,256]{3,2,1,0:T(8,128)(2,1)S(1)}, bf16[1,2,256,256]{3,2,1,0:T(8,128)(2,1)}, u32[]{:S(2)}) copy-start(bf16[1,2,256,256]{3,2,1,0:T(8,128)(2,1)} %wave_ref.1) | copy-start | bytes 786436
  2.5 0.7 copy-start.2
  32.2 1.9 %copy-start = (bf16[16,2,256,256]{3,2,1,0:T(8,128)(2,1)}, bf16[16,2,256,256]{3,2,1,0:T(8,128)(2,1)S(1)}, u32[]{:S(2)}) copy-start(bf16[16,2,256,256]{3,2,1,0:T(8,128)(2,1)S(1)} %gather.1.wave_ref) | copy-start | bytes 12582916
  34.1 16.2 %copy-start.3 = (s32[2,16]{1,0:T(2,128)S(1)}, s32[2,16]{1,0:T(2,128)}, u32[]{:S(2)}) copy-start(s32[2,16]{1,0:T(2,128)} %dims_ref.3) | copy-start | bytes 388

commit v2 on v0

v2 whole, which is shorter than its diff:
```python
import functools

import jax
import jax.numpy as jnp
from jax import lax
from jax.experimental import pallas as pl
from jax.experimental.pallas import tpu as pltpu
from jax.sharding import PartitionSpec as P

MESH = pl.DeviceIdType.MESH
GROUP = 4
LAG = 2


def chip_of(pos, chips):
    if chips == 8:
        back = pos // 4
        return 2 * (pos + back * (7 - 2 * pos)) + back
    return pos


def pos_of(chip, chips):
    if chips == 8:
        up, col = chip // 2, chip % 2
        return up + col * (7 - 2 * up)
    return chip


def places(chips):
    me = lax.axis_index("term")
    core = lax.rem(me, 2)
    pos = pos_of(me // 2, chips)

    def at(shift):
        return 2 * chip_of(lax.rem(pos + shift + chips, chips), chips) + core

    return me, core, at, me + 1 - 2 * core


def greet(devices):
    barrier = pltpu.get_barrier_semaphore()
    for device in devices:
        pl.semaphore_signal(barrier, inc=1, device_id={"term": device}, device_id_type=MESH)
    pl.semaphore_wait(barrier, len(devices))


def reach(chips, way, v):
    return chips // 2 - (1 if way != v else 0)


def kernel(chips, count, table_ref, wave_ref, left_hbm, right_hbm, out_ref,
           wave_in, lefts, rights, got0, got1, sums, own, other, shared, sent, came,
           load_sem, ag_send, ag_recv, ag_sib_send, ag_sib_recv, rs_send, rs_recv, rs_sib_send, rs_sib_recv):
    size = out_ref.shape[-1]
    half = chips // 2
    got = (got0, got1)
    me, core, at, sib = places(chips)
    flip = 1 - 2 * core
    waits = []

    def begin(copy):
        copy.start()
        waits.append(copy)

    loads = [
        pltpu.make_async_copy(wave_ref.at[0], wave_in, load_sem.at[0]),
        pltpu.make_async_copy(left_hbm, lefts, load_sem.at[1]),
        pltpu.make_async_copy(right_hbm, rights, load_sem.at[2]),
    ]
    for copy in loads:
        copy.start()
    greet((at(1), at(-1), sib))

    rows = lax.broadcasted_iota(jnp.int32, (size, size), 0)
    cols = lax.broadcasted_iota(jnp.int32, (size, size), 1)
    dims = 2 * count + 2 * chips
    inside = (rows < table_ref[dims + me]) & (cols < table_ref[dims + 2 * chips + me])
    mask = jnp.where(inside, 1.0, 0.0).astype(jnp.float32)

    def ag_ring(way, step, v, index):
        return pltpu.make_async_remote_copy(
            src_ref=got[v].at[index],
            dst_ref=got[v].at[index],
            send_sem=ag_send.at[way, step, v],
            recv_sem=ag_recv.at[way, step, v],
            device_id={"term": at(1 - 2 * way)},
            device_id_type=MESH,
        )

    def ag_sibling(way, step, v, index):
        return pltpu.make_async_remote_copy(
            src_ref=got[v].at[index],
            dst_ref=got[v].at[index],
            send_sem=ag_sib_send.at[way, step, v],
            recv_sem=ag_sib_recv.at[way, step, v],
            device_id={"term": sib},
            device_id_type=MESH,
        )

    def ag_open(v):
        got[v][me] = (wave_in[v].astype(jnp.float32) * mask).astype(jnp.bfloat16)
        for way in range(2):
            begin(ag_ring(way, 0, v, me))
        begin(ag_sibling(0, half, v, me))

    def ag_event(way, step, v):
        index = at(-(step + 1) * (1 - 2 * way))
        ag_ring(way, step, v, index).wait_recv()
        if step + 1 < reach(chips, way, v):
            begin(ag_ring(way, step + 1, v, index))
        begin(ag_sibling(way, step, v, index))

    def ag_plan(v):
        return [(way, step, v) for step in range(half) for way in (v, 1 - v) if step < reach(chips, way, v)]

    def ag_close(v):
        for way, step, _ in ag_plan(v):
            ag_sibling(way, step, v, at(-(step + 1) * (1 - 2 * way)) + flip).wait_recv()
        ag_sibling(0, half, v, me + flip).wait_recv()

    def rs_sibling(slot, v):
        return pltpu.make_async_remote_copy(
            src_ref=other.at[v, slot],
            dst_ref=shared.at[v, slot],
            send_sem=rs_sib_send.at[v, slot],
            recv_sem=rs_sib_recv.at[v, slot],
            device_id={"term": sib},
            device_id_type=MESH,
        )

    def rs_ring(way, step, v):
        return pltpu.make_async_remote_copy(
            src_ref=sent.at[way, step, v],
            dst_ref=came.at[way, step, v],
            send_sem=rs_send.at[way, step, v],
            recv_sem=rs_recv.at[way, step, v],
            device_id={"term": at(1 - 2 * way)},
            device_id_type=MESH,
        )

    def rs_plan(v):
        plan = []
        for step in range(half):
            for way in (v, 1 - v):
                first = half - reach(chips, way, v)
                if step >= first:
                    plan.append((len(plan), way, step, first, v))
        return plan

    def rs_open(v):
        places_of = [at((half - step) * (1 - 2 * way)) for _, way, step, _, _ in rs_plan(v)] + [me]
        for slot, index in enumerate(places_of):
            other[v, slot] = sums[table_ref[2 * count + index + flip]].astype(jnp.bfloat16)
            begin(rs_sibling(slot, v))
        for slot, index in enumerate(places_of):
            own[v, slot] = sums[table_ref[2 * count + index]]

    def rs_event(slot, way, step, first, v):
        rs_sibling(slot, v).wait_recv()
        total = own[v, slot] + shared[v, slot].astype(jnp.float32)
        if step > first:
            rs_ring(way, step - 1, v).wait_recv()
            total += came[way, step - 1, v].astype(jnp.float32)
        sent[way, step, v] = total.astype(jnp.bfloat16)
        begin(rs_ring(way, step, v))

    def rs_close(v):
        rs_sibling(chips - 1, v).wait_recv()
        total = own[v, chips - 1] + shared[v, chips - 1].astype(jnp.float32)
        for way in range(2):
            rs_ring(way, half - 1, v).wait_recv()
            total += came[way, half - 1, v].astype(jnp.float32)
        out_ref[0, v] = (total * mask).astype(jnp.bfloat16)

    def products(v, first, last):
        @pl.loop(first, last)
        def _(step):
            for g in range(GROUP):
                p = step * GROUP + g
                half_product = jnp.dot(
                    lefts[p], got[v][table_ref[p]], preferred_element_type=jnp.float32
                ).astype(jnp.bfloat16)
                full = lax.dot_general(
                    half_product, rights[p], (((1,), (1,)), ((), ())), preferred_element_type=jnp.float32
                )
                sums[p + 1] = full + sums[table_ref[count + p]]

    def products_beside(v, events):
        groups = count // GROUP
        cuts = [groups * i // (len(events) + 1) for i in range(len(events) + 2)]
        for i in range(len(events) + 1):
            if cuts[i + 1] > cuts[i]:
                products(v, cuts[i], cuts[i + 1])
            if i < len(events):
                events[i]()

    loads[0].wait()
    ag_open(0)
    sums[0] = jnp.zeros((size, size), jnp.float32)
    late = ag_plan(1)
    for step in range(half):
        for item in ag_plan(0):
            if item[1] == step:
                ag_event(*item)
        if step == LAG - 1:
            ag_open(1)
        if step >= LAG:
            for item in ag_plan(1):
                if item[1] == step - LAG:
                    ag_event(*item)
                    late.remove(item)
    ag_close(0)
    loads[1].wait()
    loads[2].wait()
    products_beside(0, [functools.partial(ag_event, *item) for item in late])
    rs_open(0)
    ag_close(1)
    products_beside(1, [functools.partial(rs_event, *item) for item in rs_plan(0)])
    rs_open(1)
    for item in rs_plan(1):
        rs_event(*item)
    for v in range(2):
        rs_close(v)
    for copy in waits:
        copy.wait_send()


def call(chips, table, wave, lefts, rights):
    half = chips // 2
    count, size, _ = lefts.shape
    dma = pltpu.SemaphoreType.DMA
    block = (size, size)
    anywhere = pl.BlockSpec(memory_space=pl.ANY)
    return pl.pallas_call(
        functools.partial(kernel, chips, count),
        out_shape=jax.ShapeDtypeStruct((1, 2) + block, jnp.bfloat16),
        in_specs=[pl.BlockSpec(memory_space=pltpu.SMEM), anywhere, anywhere, anywhere],
        out_specs=pl.BlockSpec(memory_space=pltpu.VMEM),
        scratch_shapes=[
            pltpu.VMEM((2,) + block, jnp.bfloat16),
            pltpu.VMEM((count,) + block, jnp.bfloat16),
            pltpu.VMEM((count,) + block, jnp.bfloat16),
            pltpu.VMEM((2 * chips,) + block, jnp.bfloat16),
            pltpu.VMEM((2 * chips,) + block, jnp.bfloat16),
            pltpu.VMEM((count + 1,) + block, jnp.float32),
            pltpu.VMEM((2, chips) + block, jnp.float32),
            pltpu.VMEM((2, chips) + block, jnp.bfloat16),
            pltpu.VMEM((2, chips) + block, jnp.bfloat16),
            pltpu.VMEM((2, half, 2) + block, jnp.bfloat16),
            pltpu.VMEM((2, half, 2) + block, jnp.bfloat16),
            dma((3,)),
            dma((2, half, 2)),
            dma((2, half, 2)),
            dma((2, half + 1, 2)),
            dma((2, half + 1, 2)),
            dma((2, half, 2)),
            dma((2, half, 2)),
            dma((2, chips)),
            dma((2, chips)),
        ],
        compiler_params=pltpu.CompilerParams(
            collective_id=0, has_side_effects=True, vmem_limit_bytes=61 * 2**20
        ),
        name="davidson",
    )(table, wave, lefts, rights)


def per_device(chips, wave, left_ops, right_ops, pair_src, pair_dst, sector_dims):
    size = wave.shape[-1]
    srcs = pair_src.reshape(-1)
    dsts = pair_dst.reshape(-1)
    count = srcs.shape[0]
    order = jnp.arange(count, dtype=jnp.int32)
    earlier = (dsts[:, None] == dsts[None, :]) & (order[None, :] < order[:, None])
    prev = jnp.max(jnp.where(earlier, order[None, :] + 1, 0), axis=1)
    ends = dsts[None, :] == jnp.arange(2 * chips, dtype=jnp.int32)[:, None]
    last = jnp.max(jnp.where(ends, order[None, :] + 1, 0), axis=1)
    table = jnp.concatenate([srcs, prev, last, sector_dims.reshape(-1)])
    return call(
        chips, table, wave, left_ops.reshape(-1, size, size), right_ops.reshape(-1, size, size)
    )


def solution(mesh):
    held = P(("mol", "term"), None, None, None)
    index = P(("mol", "term"), None)
    return jax.shard_map(
        functools.partial(per_device, mesh.shape["term"] // 2),
        mesh=mesh,
        in_specs=(held, held, held, index, index, P(None, "mol")),
        out_specs=held,
        check_vma=False,
    )
```

time: 334 us -> 78.9 us (0.24)
  waiting for transfers between devices: 219 us -> 0 us
  Pallas kernels: 0 us -> 73.8 us
  other arithmetic: 63.8 us -> 0.94 us
  matrix products: 20.5 us -> 0 us
  between operations: 13.4 us -> 0.01 us
  local copies, waits for them, and re-layouts: 16.7 us -> 3.95 us
    psum x1 -> x0, waiting for transfers between devices: 168 us -> none  [per_device(): totals = lax.psum(partial_sum, 'term')]
    pallas_call x0 -> x1, Pallas kernels: none -> 73.8 us  [call(): pl.pallas_call(functools.partial(kernel, chips, count), out_shape=jax.Sha...]
    scatter-add x1 -> x0, other arithmetic: 53 us -> none  [per_device(): partial_sum = jax.ops.segment_sum(full, dsts, num_segments=sectors)]
    all_gather x1 -> x0, waiting for transfers between devices: 50.1 us -> none  [per_device(): gathered = lax.all_gather(wave, 'term', axis=0, tiled=True)]
    dot_general x1 -> x0, matrix products: 20.5 us -> none  [per_device(): jnp.einsum('pvik,plk->pvil', half, rights, preferred_element_type=jnp.flo...]
    gather x1 -> x0, local copies, waits for them, and re-layouts: 8.54 us -> none  [per_device(): picked = jnp.take(masked, srcs, axis=0)]
    convert_element_type x3 -> x0, other arithmetic: 8.48 us -> none  [the longest x1 6.6 us: per_device(): masked = (gathered.astype(jnp.float32) * mask[:, None]).astype(jnp.bfloat16)]
    broadcast_in_dim x1 -> x0, local copies, waits for them, and re-layouts: 4.19 us -> none  [per_device(): partial_sum = jax.ops.segment_sum(full, dsts, num_segments=sectors)]
  transfers between devices with their start and end apart: 2 -> 0, of which waited for: 2 -> 0; matrix products, arithmetic and copies ran while one was open for 2% -> 0% of each run, Pallas kernels for 0% -> 0%
where the time goes in v2:
time: 78.9 us; the launch traced here: 78.7 us
  Pallas kernels  73.8 us (94%)
  local copies, waits for them, and re-layouts  3.95 us (5%)
  other arithmetic  0.94 us (1%)
    pallas_call x1, Pallas kernels, call(): pl.pallas_call(functools.partial(kernel, chips, count), out_shape=jax.Sha...  73.8 us
    unnamed x1, local copies, waits for them, and re-layouts  1.67 us

profile of v2, /device:TPU:0, one launch (start us, length us, event | category | flops | bytes accessed | tf_op | source)
XLA Modules:
  0.0 78.7 jit_solution(6923152371493841664)
XLA Ops:
  0.0 0.8 eq.28
  0.8 0.1 select_reduce_fusion.1
  0.9 0.2 select_reduce_fusion
  1.1 0.8 reshape.19
  1.8 0.8 reshape.20
  2.6 0.6 pad_add_fusion.table_ref
  3.2 73.8 %davidson.1 = bf16[1,2,256,256]{3,2,1,0:T(8,128)(2,1)} custom-call(s32[144]{0:T(256)} %pad_add_fusion.table_ref, bf16[1,2,256,256]{3,2,1,0:T(8,128)(2,1)} %wave_ref.1, bf16[48,256,256]{2,1,0:T(8,128)(2,1)} %bitcast.2, bf16[48,256,256]{2,1,0:T(8,128)(2,1)} %bitcast.3), custom_call_target="tpu_custom_call" | custom-call | tf_op jit(solution)/shard_map/davidson/pallas_call | solution.py:234
  77.0 1.7 %copy.8 = bf16[1,2,256,256]{3,2,1,0:T(8,128)(2,1)} copy(bf16[1,2,256,256]{3,2,1,0:T(8,128)(2,1)} %davidson.1) | data formatting | bytes 524288
  (1 shorter events, 0.0 us)

commit v3 on v2

--- a/solution.py
+++ b/solution.py
@@ -9,7 +9,8 @@
 
 MESH = pl.DeviceIdType.MESH
 GROUP = 4
-LAG = 2
+LAG = 1
+CUTS = 2
 
 
 def chip_of(pos, chips):
@@ -77,12 +78,15 @@
     inside = (rows < table_ref[dims + me]) & (cols < table_ref[dims + 2 * chips + me])
     mask = jnp.where(inside, 1.0, 0.0).astype(jnp.float32)
 
-    def ag_ring(way, step, v, index):
+    def cut(r):
+        return pl.ds(r * (size // CUTS), size // CUTS)
+
+    def ag_ring(way, step, v, index, r):
         return pltpu.make_async_remote_copy(
-            src_ref=got[v].at[index],
-            dst_ref=got[v].at[index],
-            send_sem=ag_send.at[way, step, v],
-            recv_sem=ag_recv.at[way, step, v],
+            src_ref=got[v].at[index, cut(r)],
+            dst_ref=got[v].at[index, cut(r)],
+            send_sem=ag_send.at[way, step, v, r],
+            recv_sem=ag_recv.at[way, step, v, r],
             device_id={"term": at(1 - 2 * way)},
             device_id_type=MESH,
         )
@@ -99,23 +103,32 @@
 
     def ag_open(v):
         got[v][me] = (wave_in[v].astype(jnp.float32) * mask).astype(jnp.bfloat16)
-        for way in range(2):
-            begin(ag_ring(way, 0, v, me))
+        for r in range(CUTS):
+            for way in range(2):
+                begin(ag_ring(way, 0, v, me, r))
         begin(ag_sibling(0, half, v, me))
 
-    def ag_event(way, step, v):
+    def ag_event(way, step, v, r):
         index = at(-(step + 1) * (1 - 2 * way))
-        ag_ring(way, step, v, index).wait_recv()
+        ag_ring(way, step, v, index, r).wait_recv()
         if step + 1 < reach(chips, way, v):
-            begin(ag_ring(way, step + 1, v, index))
-        begin(ag_sibling(way, step, v, index))
+            begin(ag_ring(way, step + 1, v, index, r))
+        if r == CUTS - 1:
+            begin(ag_sibling(way, step, v, index))
 
     def ag_plan(v):
-        return [(way, step, v) for step in range(half) for way in (v, 1 - v) if step < reach(chips, way, v)]
+        return [
+            (way, step, v, r)
+            for step in range(half)
+            for r in range(CUTS)
+            for way in (v, 1 - v)
+            if step < reach(chips, way, v)
+        ]
 
     def ag_close(v):
-        for way, step, _ in ag_plan(v):
-            ag_sibling(way, step, v, at(-(step + 1) * (1 - 2 * way)) + flip).wait_recv()
+        for way, step, _, r in ag_plan(v):
+            if r == 0:
+                ag_sibling(way, step, v, at(-(step + 1) * (1 - 2 * way)) + flip).wait_recv()
         ag_sibling(0, half, v, me + flip).wait_recv()
 
     def rs_sibling(slot, v):
@@ -128,12 +141,12 @@
             device_id_type=MESH,
         )
 
-    def rs_ring(way, step, v):
+    def rs_ring(way, step, v, r):
         return pltpu.make_async_remote_copy(
-            src_ref=sent.at[way, step, v],
-            dst_ref=came.at[way, step, v],
-            send_sem=rs_send.at[way, step, v],
-            recv_sem=rs_recv.at[way, step, v],
+            src_ref=sent.at[way, step, v, cut(r)],
+            dst_ref=came.at[way, step, v, cut(r)],
+            send_sem=rs_send.at[way, step, v, r],
+            recv_sem=rs_recv.at[way, step, v, r],
             device_id={"term": at(1 - 2 * way)},
             device_id_type=MESH,
         )
@@ -155,20 +168,32 @@
         for slot, index in enumerate(places_of):
             own[v, slot] = sums[table_ref[2 * count + index]]
 
-    def rs_event(slot, way, step, first, v):
-        rs_sibling(slot, v).wait_recv()
-        total = own[v, slot] + shared[v, slot].astype(jnp.float32)
+    def rs_event(slot, way, step, first, v, r):
+        if r == 0:
+            rs_sibling(slot, v).wait_recv()
+        total = own[v, slot, cut(r)] + shared[v, slot, cut(r)].astype(jnp.float32)
         if step > first:
-            rs_ring(way, step - 1, v).wait_recv()
-            total += came[way, step - 1, v].astype(jnp.float32)
-        sent[way, step, v] = total.astype(jnp.bfloat16)
-        begin(rs_ring(way, step, v))
+            rs_ring(way, step - 1, v, r).wait_recv()
+            total += came[way, step - 1, v, cut(r)].astype(jnp.float32)
+        sent[way, step, v, cut(r)] = total.astype(jnp.bfloat16)
+        begin(rs_ring(way, step, v, r))
+
+    def rs_events(v, steps):
+        plan = [item for item in rs_plan(v) if item[2] in steps]
+        return [
+            functools.partial(rs_event, *item, r)
+            for step in steps
+            for r in range(CUTS)
+            for item in plan
+            if item[2] == step
+        ]
 
     def rs_close(v):
         rs_sibling(chips - 1, v).wait_recv()
         total = own[v, chips - 1] + shared[v, chips - 1].astype(jnp.float32)
         for way in range(2):
-            rs_ring(way, half - 1, v).wait_recv()
+            for r in range(CUTS):
+                rs_ring(way, half - 1, v, r).wait_recv()
             total += came[way, half - 1, v].astype(jnp.float32)
         out_ref[0, v] = (total * mask).astype(jnp.bfloat16)
 
@@ -215,10 +240,15 @@
     products_beside(0, [functools.partial(ag_event, *item) for item in late])
     rs_open(0)
     ag_close(1)
-    products_beside(1, [functools.partial(rs_event, *item) for item in rs_plan(0)])
+    early = half // 2 + 1
+    products_beside(1, rs_events(0, range(early)))
     rs_open(1)
-    for item in rs_plan(1):
-        rs_event(*item)
+    for step in range(half):
+        if step + early < half:
+            for event in rs_events(0, [step + early]):
+                event()
+        for event in rs_events(1, [step]):
+            event()
     for v in range(2):
         rs_close(v)
     for copy in waits:
@@ -249,12 +279,12 @@
             pltpu.VMEM((2, half, 2) + block, jnp.bfloat16),
             pltpu.VMEM((2, half, 2) + block, jnp.bfloat16),
             dma((3,)),
-            dma((2, half, 2)),
-            dma((2, half, 2)),
+            dma((2, half, 2, CUTS)),
+            dma((2, half, 2, CUTS)),
             dma((2, half + 1, 2)),
             dma((2, half + 1, 2)),
-            dma((2, half, 2)),
-            dma((2, half, 2)),
+            dma((2, half, 2, CUTS)),
+            dma((2, half, 2, CUTS)),
             dma((2, chips)),
             dma((2, chips)),
         ],

time: 78.9 us -> 72.6 us (0.920)
  Pallas kernels: 73.8 us -> 67.5 us
    pallas_call x1, Pallas kernels: 73.8 us -> 67.5 us  [call(): pl.pallas_call(functools.partial(kernel, chips, count), out_shape=jax.Sha...]
where the time goes in v3:
time: 72.6 us; the launch traced here: 72.4 us
  Pallas kernels  67.5 us (93%)
  local copies, waits for them, and re-layouts  3.95 us (5%)
  other arithmetic  0.94 us (1%)
    pallas_call x1, Pallas kernels, call(): pl.pallas_call(functools.partial(kernel, chips, count), out_shape=jax.Sha...  67.5 us
    unnamed x1, local copies, waits for them, and re-layouts  1.67 us

profile of v3, /device:TPU:0, one launch (start us, length us, event | category | flops | bytes accessed | tf_op | source)
XLA Modules:
  0.0 72.4 jit_solution(907042467257211818)
XLA Ops:
  0.0 0.8 %eq.28 = s32[48]{0:T(128)S(1)} reshape(s32[2,24]{1,0:T(2,128)} %param.10) | data formatting | bytes 384 | tf_op jit(solution)/shard_map/eq | solution.py:304
  0.8 0.1 select_reduce_fusion.1
  0.9 0.2 select_reduce_fusion
  1.1 0.8 %reshape.19 = s32[48]{0:T(128)S(1)} reshape(s32[2,24]{1,0:T(2,128)} %param.9) | data formatting | bytes 384 | tf_op jit(solution)/shard_map/reshape | solution.py:300
  1.8 0.8 %reshape.20 = s32[32]{0:T(128)S(1)} reshape(s32[2,16]{1,0:T(2,128)} %param.11) | data formatting | bytes 256 | tf_op jit(solution)/shard_map/reshape | solution.py:308
  2.6 0.6 pad_add_fusion.table_ref
  3.2 67.5 %davidson.1 = bf16[1,2,256,256]{3,2,1,0:T(8,128)(2,1)} custom-call(s32[144]{0:T(256)} %pad_add_fusion.table_ref, bf16[1,2,256,256]{3,2,1,0:T(8,128)(2,1)} %wave_ref.1, bf16[48,256,256]{2,1,0:T(8,128)(2,1)} %bitcast.2, bf16[48,256,256]{2,1,0:T(8,128)(2,1)} %bitcast.3), custom_call_target="tpu_custom_call" | custom-call | tf_op jit(solution)/shard_map/davidson/pallas_call | solution.py:264
  70.7 1.7 %copy.8 = bf16[1,2,256,256]{3,2,1,0:T(8,128)(2,1)} copy(bf16[1,2,256,256]{3,2,1,0:T(8,128)(2,1)} %davidson.1) | data formatting | bytes 524288
  (1 shorter events, 0.0 us)

commit v4 on v3

--- a/solution.py
+++ b/solution.py
@@ -10,7 +10,7 @@
 MESH = pl.DeviceIdType.MESH
 GROUP = 4
 LAG = 1
-CUTS = 2
+CUTS = 4
 
 
 def chip_of(pos, chips):
@@ -49,7 +49,7 @@
     return chips // 2 - (1 if way != v else 0)
 
 
-def kernel(chips, count, table_ref, wave_ref, left_hbm, right_hbm, out_ref,
+def kernel(chips, count, src_ref, dims_ref, table_ref, wave_ref, left_hbm, right_hbm, out_ref,
            wave_in, lefts, rights, got0, got1, sums, own, other, shared, sent, came,
            load_sem, ag_send, ag_recv, ag_sib_send, ag_sib_recv, rs_send, rs_recv, rs_sib_send, rs_sib_recv):
     size = out_ref.shape[-1]
@@ -57,6 +57,7 @@
     got = (got0, got1)
     me, core, at, sib = places(chips)
     flip = 1 - 2 * core
+    row = src_ref.shape[1]
     waits = []
 
     def begin(copy):
@@ -74,8 +75,7 @@
 
     rows = lax.broadcasted_iota(jnp.int32, (size, size), 0)
     cols = lax.broadcasted_iota(jnp.int32, (size, size), 1)
-    dims = 2 * count + 2 * chips
-    inside = (rows < table_ref[dims + me]) & (cols < table_ref[dims + 2 * chips + me])
+    inside = (rows < dims_ref[0, me]) & (cols < dims_ref[1, me])
     mask = jnp.where(inside, 1.0, 0.0).astype(jnp.float32)
 
     def cut(r):
@@ -163,10 +163,10 @@
     def rs_open(v):
         places_of = [at((half - step) * (1 - 2 * way)) for _, way, step, _, _ in rs_plan(v)] + [me]
         for slot, index in enumerate(places_of):
-            other[v, slot] = sums[table_ref[2 * count + index + flip]].astype(jnp.bfloat16)
+            other[v, slot] = sums[table_ref[count + index + flip]].astype(jnp.bfloat16)
             begin(rs_sibling(slot, v))
         for slot, index in enumerate(places_of):
-            own[v, slot] = sums[table_ref[2 * count + index]]
+            own[v, slot] = sums[table_ref[count + index]]
 
     def rs_event(slot, way, step, first, v, r):
         if r == 0:
@@ -203,12 +203,12 @@
             for g in range(GROUP):
                 p = step * GROUP + g
                 half_product = jnp.dot(
-                    lefts[p], got[v][table_ref[p]], preferred_element_type=jnp.float32
+                    lefts[p], got[v][src_ref[p // row, lax.rem(p, row)]], preferred_element_type=jnp.float32
                 ).astype(jnp.bfloat16)
                 full = lax.dot_general(
                     half_product, rights[p], (((1,), (1,)), ((), ())), preferred_element_type=jnp.float32
                 )
-                sums[p + 1] = full + sums[table_ref[count + p]]
+                sums[p + 1] = full + sums[table_ref[p]]
 
     def products_beside(v, events):
         groups = count // GROUP
@@ -240,7 +240,7 @@
     products_beside(0, [functools.partial(ag_event, *item) for item in late])
     rs_open(0)
     ag_close(1)
-    early = half // 2 + 1
+    early = half // 2
     products_beside(1, rs_events(0, range(early)))
     rs_open(1)
     for step in range(half):
@@ -255,7 +255,7 @@
         copy.wait_send()
 
 
-def call(chips, table, wave, lefts, rights):
+def call(chips, srcs, dims, table, wave, lefts, rights):
     half = chips // 2
     count, size, _ = lefts.shape
     dma = pltpu.SemaphoreType.DMA
@@ -264,7 +264,7 @@
     return pl.pallas_call(
         functools.partial(kernel, chips, count),
         out_shape=jax.ShapeDtypeStruct((1, 2) + block, jnp.bfloat16),
-        in_specs=[pl.BlockSpec(memory_space=pltpu.SMEM), anywhere, anywhere, anywhere],
+        in_specs=[pl.BlockSpec(memory_space=pltpu.SMEM)] * 3 + [anywhere] * 3,
         out_specs=pl.BlockSpec(memory_space=pltpu.VMEM),
         scratch_shapes=[
             pltpu.VMEM((2,) + block, jnp.bfloat16),
@@ -292,22 +292,27 @@
             collective_id=0, has_side_effects=True, vmem_limit_bytes=61 * 2**20
         ),
         name="davidson",
-    )(table, wave, lefts, rights)
+    )(srcs, dims, table, wave, lefts, rights)
 
 
 def per_device(chips, wave, left_ops, right_ops, pair_src, pair_dst, sector_dims):
     size = wave.shape[-1]
-    srcs = pair_src.reshape(-1)
     dsts = pair_dst.reshape(-1)
-    count = srcs.shape[0]
+    count = dsts.shape[0]
     order = jnp.arange(count, dtype=jnp.int32)
     earlier = (dsts[:, None] == dsts[None, :]) & (order[None, :] < order[:, None])
     prev = jnp.max(jnp.where(earlier, order[None, :] + 1, 0), axis=1)
     ends = dsts[None, :] == jnp.arange(2 * chips, dtype=jnp.int32)[:, None]
     last = jnp.max(jnp.where(ends, order[None, :] + 1, 0), axis=1)
-    table = jnp.concatenate([srcs, prev, last, sector_dims.reshape(-1)])
+    table = jnp.concatenate([prev, last])
     return call(
-        chips, table, wave, left_ops.reshape(-1, size, size), right_ops.reshape(-1, size, size)
+        chips,
+        pair_src,
+        sector_dims,
+        table,
+        wave,
+        left_ops.reshape(-1, size, size),
+        right_ops.reshape(-1, size, size),
     )
 
 

time: 72.6 us -> 69.3 us (0.955)
  Pallas kernels: 67.5 us -> 65.8 us
  local copies, waits for them, and re-layouts: 3.95 us -> 2.43 us
    pallas_call x1, Pallas kernels: 67.5 us -> 65.8 us  [call(): pl.pallas_call(functools.partial(kernel, chips, count), out_shape=jax.Sha...]
    reshape x2 -> x0, local copies, waits for them, and re-layouts: 1.52 us -> none  [the longest x1 0.76 us: per_device(): srcs = pair_src.reshape(-1)]
where the time goes in v4:
time: 69.3 us; the launch traced here: 69.2 us
  Pallas kernels  65.8 us (95%)
  local copies, waits for them, and re-layouts  2.43 us (4%)
  other arithmetic  0.89 us (1%)
    pallas_call x1, Pallas kernels, call(): pl.pallas_call(functools.partial(kernel, chips, count), out_shape=jax.Sha...  65.8 us
    unnamed x1, local copies, waits for them, and re-layouts  1.67 us

profile of v4, /device:TPU:0, one launch (start us, length us, event | category | flops | bytes accessed | tf_op | source)
XLA Modules:
  0.0 69.2 jit_solution(18107227867823010850)
XLA Ops:
  0.0 0.8 %eq.28 = s32[48]{0:T(128)S(1)} reshape(s32[2,24]{1,0:T(2,128)} %param.10) | data formatting | bytes 384 | tf_op jit(solution)/shard_map/eq | solution.py:303
  0.8 0.1 select_reduce_fusion.1
  0.9 0.2 select_reduce_fusion
  1.1 0.6 pad_add_fusion.table_ref
  1.7 65.8 %davidson.1 = bf16[1,2,256,256]{3,2,1,0:T(8,128)(2,1)} custom-call(s32[2,24]{1,0:T(2,128)} %src_ref.1, s32[2,16]{1,0:T(2,128)} %dims_ref.1, s32[64]{0:T(128)} %pad_add_fusion.table_ref, bf16[1,2,256,256]{3,2,1,0:T(8,128)(2,1)} %wave_ref.1, bf16[48,256,256]{2,1,0:T(8,128)(2,1)} %bitcast.2, bf16[48,256,256]{2,1,0:T(8,128)(2,1)} %bitcast.3), custom_call_target="tpu_custom_call" | custom-call | tf_op jit(solution)/shard_map/davidson/pallas_call | solution.py:264
  67.5 1.7 %copy.8 = bf16[1,2,256,256]{3,2,1,0:T(8,128)(2,1)} copy(bf16[1,2,256,256]{3,2,1,0:T(8,128)(2,1)} %davidson.1) | data formatting | bytes 524288
  (1 shorter events, 0.0 us)
